TPU v7x, 32 devices: a whole 2x2x4 slice. The times are simulated.
32 devices in a mesh: gx: 4 (over y, x), gy: 4 (over z), col: 2 (over core).
Axes of the slice: x: 2, y: 2, z: 4, core: 2. Of those that a mesh axis runs over, the one named last changes fastest.
Arguments:
- density: float32 [10, 10, 10, 16, 512], P('col', None, None, 'gx', 'gy'), may hold values from -6 to 6
- velocity: float32 [2, 16, 512], P(None, 'gx', 'gy'), may hold values from -3 to 3
- shear_rates: float32 [4, 16, 512], P(None, 'gx', 'gy'), may hold values from -4 to 4
- hermite_matrix: float32 [10, 10], replicated, may hold values from -2 to 2
- laguerre_matrix: float32 [10, 10], replicated, may hold values from -2 to 2
- flow_first: float32 [4, 10, 10], replicated, may hold values from -2 to 2
- flow_second: float32 [4, 10, 10], replicated, may hold values from -2 to 2
- stress_weights: float32 [3, 10, 10, 10], P(None, 'col'), may hold values from -0.1875 to 0.1875
Outputs:
- advanced: float32 [10, 10, 10, 16, 512], P('col', None, None, 'gx', 'gy')
- stress: float32 [3, 16, 512], P(None, 'gx', 'gy')
All inputs are finite; a program needn't handle non-finite values.
Results may differ from a plain program's by a relative error of at most 0.0003.
Values sent between devices are 32-bit elements; how exact they have to be, the bound alone decides.
A program may use at most 128 MiB of HBM per device.

v0:
```python
import functools

import jax
import jax.numpy as jnp
from jax import lax
from jax.experimental import pallas as pl
from jax.experimental.pallas import tpu as pltpu
from jax.sharding import PartitionSpec as P

time_step = 0.1
highest = lax.Precision.HIGHEST
MESH = pl.DeviceIdType.MESH

P_HERE = 5
HM = 10
QR = 100
WX = 4
WY = 128
ROWS = P_HERE * QR * WX
PQ = 56
GROUPS, PER = 10, 25
EARLY = 3


def dot(a, b):
    return jnp.dot(a, b, precision=highest, preferred_element_type=jnp.float32)


def tenth(i):
    return lax.shift_right_logical(i * 205, 11)


def iota(shape, axis):
    return lax.broadcasted_iota(jnp.int32, shape, axis)


def one(cond):
    return jnp.where(cond, 1.0, 0.0).astype(jnp.float32)


def kernel(nx, ny, dens_hbm, vel, shear, herm, lag, ff, fs, sw, out_hbm, stress_out,
           dens, other, acc, send_lo, send_hi, recv_lo, recv_hi, rim, rim_lo, rim_hi,
           xs, wmat, kqr, mom, mom_lo, mom_hi, part, part_other,
           load_sem, out_sem, xs_send, xs_recv, col_sem, z_send, z_recv, m_send, m_recv, s_sem):
    gx, gy, col = lax.axis_index("gx"), lax.axis_index("gy"), lax.axis_index("col")
    x_next, x_prev = lax.rem(gx + 1, nx), lax.rem(gx + nx - 1, nx)
    y_next, y_prev = lax.rem(gy + 1, ny), lax.rem(gy + ny - 1, ny)
    to_next, to_prev = (x_next, gy, col), (x_prev, gy, col)
    to_up, to_down = (gx, y_next, col), (gx, y_prev, col)
    to_col = (gx, gy, 1 - col)

    loads = [pltpu.make_async_copy(dens_hbm.at[pl.ds(p * 400, 400)], dens.at[pl.ds(p * 400, 400)],
                                   load_sem.at[p]) for p in range(P_HERE)]
    for c in loads:
        c.start()
    barrier = pltpu.get_barrier_semaphore()
    for d in (to_next, to_prev, to_up, to_down, to_col):
        pl.semaphore_signal(barrier, inc=1, device_id=d, device_id_type=MESH)

    def remote(src, dst, ss, rs, dev):
        return pltpu.make_async_remote_copy(src_ref=src, dst_ref=dst, send_sem=ss, recv_sem=rs,
                                            device_id=dev, device_id_type=MESH)

    x_copies = []
    for p in range(P_HERE):
        piece = pl.ds(p * 200, 200)
        x_copies.append((
            remote(send_hi.at[piece], recv_lo.at[piece], xs_send.at[0, p], xs_recv.at[0, p], to_next),
            remote(send_lo.at[piece], recv_hi.at[piece], xs_send.at[1, p], xs_recv.at[1, p], to_prev)))
    col_copy = remote(dens, other, col_sem.at[0], col_sem.at[1], to_col)
    z_copies = (remote(rim, rim_lo, z_send.at[0], z_recv.at[0], to_up),
                remote(rim, rim_hi, z_send.at[1], z_recv.at[1], to_down))
    m_copies = (remote(mom, mom_lo, m_send.at[0], m_recv.at[0], to_next),
                remote(mom, mom_hi, m_send.at[1], m_recv.at[1], to_prev))
    s_copy = remote(part, part_other, s_sem.at[0], s_sem.at[1], to_col)

    for p in range(P_HERE):
        loads[p].wait()
        for j in range(2):
            rows = pl.ds(p * 200 + j, QR, stride=2)
            send_lo[rows, :] = dens[pl.ds(p * 400 + j, QR, stride=WX), :]
            send_hi[rows, :] = dens[pl.ds(p * 400 + 2 + j, QR, stride=WX), :]
        if p == 0:
            pl.semaphore_wait(barrier, 5)
        if p < EARLY:
            for c in x_copies[p]:
                c.start()
    col_copy.start()

    lane = iota((8, WY), 1)

    def pack(g, _):
        tile = jnp.zeros((8, WY), jnp.float32)
        for k in range(PER):
            f = dens[pl.ds(pl.multiple_of(g * (8 * PER), 8) + 8 * k, 8), :]
            tile = jnp.where((lane >> 2) == k, pltpu.roll(f, (4 * k + 2) % WY, 1), tile)
        rim[pl.ds(pl.multiple_of(g * 8, 8), 8), :] = tile
        return 0

    lax.fori_loop(0, GROUPS, pack, 0)
    for c in z_copies:
        c.start()

    row, hot = iota((QR, HM), 0), iota((QR, HM), 1)
    row_t, hot_t = iota((HM, QR), 1), iota((HM, QR), 0)
    rr, cc = iota((QR, QR), 0), iota((QR, QR), 1)
    rq, cq = tenth(rr), tenth(cc)
    h_exp = dot(dot(one(tenth(row) == hot), herm[...]), one(tenth(row_t) == hot_t))
    l_exp = dot(dot(one(row - 10 * tenth(row) == hot), lag[...]), one(row_t - 10 * tenth(row_t) == hot_t))
    kqr[...] = time_step * (jnp.where(rr - 10 * rq == cc - 10 * cq, h_exp, 0.0) + jnp.where(rq == cq, l_exp, 0.0))

    def cells(tile, x):
        return tile[:, x * WY:(x + 1) * WY]

    u_pos = [-time_step * jnp.maximum(vel[0, x:x + 1, :], 0.0) for x in range(WX)]
    u_neg = [-time_step * jnp.minimum(vel[0, x:x + 1, :], 0.0) for x in range(WX)]

    mom[...] = jnp.zeros_like(mom)

    def own(p, _):
        c = [dens[pl.ds(p * 400 + x, QR, stride=WX), :] for x in range(WX)]
        block = jnp.concatenate(c, axis=1)
        rate = dot(kqr[...], block)
        mom[0:3, :] += dot(sw[p], block)
        for x in range(WX):
            value = cells(rate, x) + (1.5 * (u_pos[x] - u_neg[x])) * c[x]
            if x >= 1:
                value += (-2.0 * u_pos[x]) * c[x - 1]
            if x >= 2:
                value += (0.5 * u_pos[x]) * c[x - 2]
            if x < WX - 1:
                value += (2.0 * u_neg[x]) * c[x + 1]
            if x < WX - 2:
                value += (-0.5 * u_neg[x]) * c[x + 2]
            acc[pl.ds(p * 400 + x, QR, stride=WX), :] = value
        return 0

    lax.fori_loop(0, P_HERE, own, 0)
    for c in m_copies:
        c.start()
    for p in range(EARLY, P_HERE):
        for c in x_copies[p]:
            c.start()

    my0, other0 = col * P_HERE, (1 - col) * P_HERE
    r1, k1 = iota((PQ, 40), 0), iota((PQ, 40), 1)
    r1h, k1h = iota((PQ, HM), 0), iota((PQ, HM), 1)
    c2, j2 = iota((HM, 2 * PQ), 1), iota((HM, 2 * PQ), 0)
    near = c2 < PQ
    c2 = jnp.where(near, c2, c2 - PQ)
    real = c2 < 50
    p_hot = one(real & (j2 == jnp.where(near, my0, other0) + tenth(c2)))
    q_hot = one(real & (j2 == c2 - 10 * tenth(c2)))
    b_hot = one((r1h < 50) & (k1h == r1h - 10 * tenth(r1h)))
    a_hot = one((r1h < 50) & (k1h == my0 + tenth(r1h)))
    wmat[0:PQ, :] = time_step * dot(dot(a_hot, herm[...]), p_hot) * dot(b_hot, q_hot)
    for c in range(4):
        a_c = one((r1 < 50) & (k1 == 4 * (my0 + tenth(r1)) + c))
        b_c = one((r1 < 50) & (k1 == 4 * (r1 - 10 * tenth(r1)) + c))
        wmat[(c + 1) * PQ:(c + 2) * PQ, :] = time_step * (
            dot(dot(a_c, ff[...]), p_hot) * dot(dot(b_c, fs[...]), q_hot))
    xs[...] = jnp.zeros_like(xs)

    for c in z_copies:
        c.wait_recv()
    v = jnp.concatenate([vel[1], vel[1]], axis=0)
    v_pos = -time_step * jnp.maximum(v, 0.0)
    v_neg = -time_step * jnp.minimum(v, 0.0)
    k_0 = 1.0 + 1.5 * (v_pos - v_neg)
    k_m1, k_m2, k_p1, k_p2 = -2.0 * v_pos, 0.5 * v_pos, 2.0 * v_neg, -0.5 * v_neg
    low_wall = jnp.where(gy == 0, 0.0, 1.0).astype(jnp.float32)
    high_wall = jnp.where(gy == ny - 1, 0.0, 1.0).astype(jnp.float32)

    def normal(g, _):
        at = pl.ds(pl.multiple_of(g * 8, 8), 8)
        rims = jnp.where((lane & 3) < 2, rim_lo[at, :] * low_wall, rim_hi[at, :] * high_wall)
        for k in range(PER):
            here = pl.ds(pl.multiple_of(g * (8 * PER), 8) + 8 * k, 8)
            f = dens[here, :]
            h = pltpu.roll(rims, (2 * WY - 4 * k - 2) % WY, 1)
            m1 = pltpu.roll(jnp.where(lane == WY - 1, h, f), 1, 1)
            m2 = pltpu.roll(jnp.where(lane >= WY - 2, h, f), 2, 1)
            p1 = pltpu.roll(jnp.where(lane == 0, h, f), WY - 1, 1)
            p2 = pltpu.roll(jnp.where(lane < 2, h, f), WY - 2, 1)
            acc[here, :] += k_0 * f + k_m1 * m1 + k_m2 * m2 + k_p1 * p1 + k_p2 * p2
        return 0

    lax.fori_loop(0, GROUPS, normal, 0)

    col_copy.wait_recv()

    def couple(r, _):
        for x in range(WX):
            rows = pl.ds(r * WX + x, 50, stride=40)
            xs[0:50, x * WY:(x + 1) * WY] = dens[rows, :]
            xs[PQ:PQ + 50, x * WY:(x + 1) * WY] = other[rows, :]
        t = dot(wmat[...], xs[...])
        for x in range(WX):
            value = cells(t, x)[0:50]
            for c in range(4):
                value += shear[c, x:x + 1, :] * cells(t, x)[(c + 1) * PQ:(c + 1) * PQ + 50]
            acc[pl.ds(r * WX + x, 50, stride=40), :] += value
        return 0

    lax.fori_loop(0, HM, couple, 0)

    part[...] = jnp.zeros_like(part)

    def moments(p, _):
        block = jnp.concatenate([acc[pl.ds(p * 400 + x, QR, stride=WX), :] for x in range(WX)], axis=1)
        part[0:3, :] += dot(sw[p], block)
        return 0

    lax.fori_loop(0, P_HERE, moments, 0)
    for c in m_copies:
        c.wait_recv()

    def edges(lo2, lo1, hi0, hi1):
        return ((-2.0 * u_pos[0]) * lo1 + (0.5 * u_pos[0]) * lo2,
                (0.5 * u_pos[1]) * lo1,
                (-0.5 * u_neg[2]) * hi0,
                (2.0 * u_neg[3]) * hi0 + (-0.5 * u_neg[3]) * hi1)

    rims = edges(cells(mom_lo, 2), cells(mom_lo, 3), cells(mom_hi, 0), cells(mom_hi, 1))
    for x in range(WX):
        part[:, x * WY:(x + 1) * WY] += rims[x]
    s_copy.start()

    outs = []
    for p in range(P_HERE):
        for c in x_copies[p]:
            c.wait_recv()
        lo2, lo1 = (recv_lo[pl.ds(p * 200 + j, QR, stride=2), :] for j in range(2))
        hi0, hi1 = (recv_hi[pl.ds(p * 200 + j, QR, stride=2), :] for j in range(2))
        add = edges(lo2, lo1, hi0, hi1)
        for x in range(WX):
            acc[pl.ds(p * 400 + x, QR, stride=WX), :] += add[x]
        out = pltpu.make_async_copy(acc.at[pl.ds(p * 400, 400)], out_hbm.at[pl.ds(p * 400, 400)], out_sem.at[p])
        out.start()
        outs.append(out)
    s_copy.wait_recv()
    total = part[...] + part_other[...]
    for x in range(WX):
        stress_out[:, x, :] = cells(total, x)[0:3]
    for pair in x_copies + [z_copies, m_copies, (col_copy, s_copy)]:
        for c in pair:
            c.wait_send()
    for out in outs:
        out.wait()


def body(nx, ny, density, velocity, shear_rates, hermite_matrix, laguerre_matrix, flow_first,
         flow_second, stress_weights):
    assert density.shape == (P_HERE, HM, HM, WX, WY)
    f32 = jnp.float32
    vmem = pl.BlockSpec(memory_space=pltpu.VMEM)
    hbm = pl.BlockSpec(memory_space=pl.ANY)
    dma = pltpu.SemaphoreType.DMA
    advanced, stress = pl.pallas_call(
        functools.partial(kernel, nx, ny),
        out_shape=(jax.ShapeDtypeStruct((ROWS, WY), f32), jax.ShapeDtypeStruct((3, WX, WY), f32)),
        in_specs=[hbm] + [vmem] * 7,
        out_specs=(hbm, vmem),
        scratch_shapes=[
            pltpu.VMEM((ROWS, WY), f32), pltpu.VMEM((ROWS, WY), f32), pltpu.VMEM((ROWS, WY), f32),
            pltpu.VMEM((ROWS // 2, WY), f32), pltpu.VMEM((ROWS // 2, WY), f32),
            pltpu.VMEM((ROWS // 2, WY), f32), pltpu.VMEM((ROWS // 2, WY), f32),
            pltpu.VMEM((8 * GROUPS, WY), f32), pltpu.VMEM((8 * GROUPS, WY), f32), pltpu.VMEM((8 * GROUPS, WY), f32),
            pltpu.VMEM((2 * PQ, WX * WY), f32), pltpu.VMEM((5 * PQ, 2 * PQ), f32), pltpu.VMEM((QR, QR), f32),
            pltpu.VMEM((8, WX * WY), f32), pltpu.VMEM((8, WX * WY), f32), pltpu.VMEM((8, WX * WY), f32),
            pltpu.VMEM((8, WX * WY), f32), pltpu.VMEM((8, WX * WY), f32),
            dma((P_HERE,)), dma((P_HERE,)), dma((2, P_HERE)), dma((2, P_HERE)), dma((2,)),
            dma((2,)), dma((2,)), dma((2,)), dma((2,)), dma((2,)),
        ],
        compiler_params=pltpu.CompilerParams(collective_id=0, has_side_effects=True,
                                             vmem_limit_bytes=32 * 1024 * 1024),
        cost_estimate=pl.CostEstimate(flops=600_000_000, bytes_accessed=3_000_000, transcendentals=0),
    )(
        density.reshape(ROWS, WY), velocity, shear_rates, hermite_matrix, laguerre_matrix,
        flow_first.transpose(1, 0, 2).reshape(4 * HM, HM), flow_second.transpose(1, 0, 2).reshape(4 * HM, HM),
        stress_weights.reshape(3, P_HERE, QR).transpose(1, 0, 2),
    )
    return advanced.reshape(density.shape), stress


def solution(mesh):
    in_specs = (
        P("col", None, None, "gx", "gy"),
        P(None, "gx", "gy"),
        P(None, "gx", "gy"),
        P(),
        P(),
        P(),
        P(),
        P(None, "col", None, None),
    )
    out_specs = (P("col", None, None, "gx", "gy"), P(None, "gx", "gy"))
    one_device = functools.partial(body, mesh.shape["gx"], mesh.shape["gy"])
    return jax.shard_map(one_device, mesh=mesh, in_specs=in_specs, out_specs=out_specs, check_vma=False)
```

profile of v0, /device:TPU:0, one launch (start us, length us, event | category | flops | bytes accessed | tf_op | source)
XLA Modules:
  0.0 36.8 jit_solution(13944316300131714651)
XLA Ops:
  0.6 0.9 %copy.11 = f32[3,5,10,10]{3,2,0,1:T(8,128)S(1)} copy(f32[3,5,10,10]{3,0,2,1:T(4,128)} %param.15) | data formatting | bytes 12000 | tf_op args[7]
  1.5 0.0 copy-start.1
  1.6 0.0 copy-start.2
  1.6 0.0 copy-start.3
  1.6 0.0 copy-start.4
  1.6 0.0 copy-start.5
  1.6 0.0 copy-start.6
  1.6 0.1 reshape.22
  1.7 0.6 %copy-done.1 = f32[4,10,10]{2,0,1:T(4,128)S(1)} copy-done((f32[4,10,10]{2,0,1:T(4,128)S(1)}, f32[4,10,10]{2,0,1:T(4,128)}, u32[]{:S(2)}) %copy-start.1) | copy-done | bytes 1624
  2.3 0.0 copy-done.2
  2.3 0.0 copy-done.3
  2.3 0.0 copy-done.4
  2.3 0.0 copy-done.5
  2.3 0.0 copy-done.6
  2.3 0.0 copy-start
  2.3 1.2 %copy-done = f32[5,10,10,4,128]{4,3,2,1,0:T(4,128)S(1)} copy-done((f32[5,10,10,4,128]{4,3,2,1,0:T(4,128)S(1)}, f32[5,10,10,4,128]{4,3,2,1,0:T(4,128)}, u32[]{:S(2)}) %copy-start) | copy-done | bytes 1024024
  3.5 31.7 %shard_map.95 = (f32[2000,128]{1,0:T(8,128)S(1)}, f32[3,4,128]{2,1,0:T(4,128)S(1)}) custom-call(f32[2000,128]{1,0:T(8,128)S(1)} %bitcast.13, f32[2,4,128]{2,1,0:T(4,128)S(1)} %copy-done.6, f32[4,4,128]{2,1,0:T(4,128)S(1)} %copy-done.3, f32[10,10]{1,0:T(8,128)S(1)} %copy-done.4, f32[10,10]{1,0:T(8,128)S(1)} %copy-done.5, f32[40,10]{1,0:T(8,128)S(1)} %bitcast.14, ...), custom_call_target="tpu_custom_call" | custom-call | flops 600000000 | bytes 3000000 | tf_op jit(solution)/shard_map/pallas_call | solution.py:259
  35.2 1.0 %copy.14 = f32[5,10,10,4,128]{4,3,2,1,0:T(4,128)} copy(f32[5,10,10,4,128]{4,3,2,1,0:T(4,128)S(1)} %bitcast.11) | data formatting | bytes 2048000
  36.2 0.6 %copy.15 = f32[3,4,128]{2,1,0:T(4,128)} copy(f32[3,4,128]{2,1,0:T(4,128)S(1)} %get-tuple-element.9) | data formatting | bytes 12288
Async XLA Ops:
  1.5 0.7 %copy-start.1 = (f32[4,10,10]{2,0,1:T(4,128)S(1)}, f32[4,10,10]{2,0,1:T(4,128)}, u32[]{:S(2)}) copy-start(f32[4,10,10]{2,0,1:T(4,128)} %param.13) | copy-start | bytes 4804
  1.6 0.7 %copy-start.2 = (f32[4,10,10]{2,0,1:T(4,128)S(1)}, f32[4,10,10]{2,0,1:T(4,128)}, u32[]{:S(2)}) copy-start(f32[4,10,10]{2,0,1:T(4,128)} %param.14) | copy-start | bytes 4804
  1.6 0.7 %copy-start.3 = (f32[4,4,128]{2,1,0:T(4,128)S(1)}, f32[4,4,128]{2,1,0:T(4,128)}, u32[]{:S(2)}) copy-start(f32[4,4,128]{2,1,0:T(4,128)} %shear.1) | copy-start | bytes 24580
  1.6 0.7 %copy-start.4 = (f32[10,10]{1,0:T(8,128)S(1)}, f32[10,10]{1,0:T(8,128)}, u32[]{:S(2)}) copy-start(f32[10,10]{1,0:T(8,128)} %herm.1) | copy-start | bytes 1204
  1.6 0.7 %copy-start.5 = (f32[10,10]{1,0:T(8,128)S(1)}, f32[10,10]{1,0:T(8,128)}, u32[]{:S(2)}) copy-start(f32[10,10]{1,0:T(8,128)} %lag.1) | copy-start | bytes 1204
  1.6 0.7 %copy-start.6 = (f32[2,4,128]{2,1,0:T(4,128)S(1)}, f32[2,4,128]{2,1,0:T(4,128)}, u32[]{:S(2)}) copy-start(f32[2,4,128]{2,1,0:T(4,128)} %vel.1) | copy-start | bytes 12292
  2.3 1.2 %copy-start = (f32[5,10,10,4,128]{4,3,2,1,0:T(4,128)S(1)}, f32[5,10,10,4,128]{4,3,2,1,0:T(4,128)}, u32[]{:S(2)}) copy-start(f32[5,10,10,4,128]{4,3,2,1,0:T(4,128)} %param.8) | copy-start | bytes 3072004
where the time goes:
time: 37 us; the launch traced here: 36.8 us
  Pallas kernels  31.7 us (86%)
  local copies, waits for them, and re-layouts  4.4 us (12%)
  between operations  0.7 us (2%)
    pallas_call x1, Pallas kernels, body(): pl.pallas_call(functools.partial(kernel, nx, ny), out_shape=(jax.ShapeDty...  31.7 us
    unnamed x17, local copies, waits for them, and re-layouts  4.3 us

commit v1 on v0

--- a/solution.py
+++ b/solution.py
@@ -18,8 +18,10 @@
 WY = 128
 ROWS = P_HERE * QR * WX
 PQ = 56
+WR = 288
 GROUPS, PER = 10, 25
-EARLY = 3
+EARLY = 4
+LAST = P_HERE - 1
 
 
 def dot(a, b):
@@ -38,10 +40,46 @@
     return jnp.where(cond, 1.0, 0.0).astype(jnp.float32)
 
 
-def kernel(nx, ny, dens_hbm, vel, shear, herm, lag, ff, fs, sw, out_hbm, stress_out,
-           dens, other, acc, send_lo, send_hi, recv_lo, recv_hi, rim, rim_lo, rim_hi,
-           xs, wmat, kqr, mom, mom_lo, mom_hi, part, part_other,
-           load_sem, out_sem, xs_send, xs_recv, col_sem, z_send, z_recv, m_send, m_recv, s_sem):
+def halves(a):
+    hi = a.astype(jnp.bfloat16)
+    return hi, (a - hi.astype(jnp.float32)).astype(jnp.bfloat16)
+
+
+def dot3(a_hi, a_lo, b):
+    b_hi, b_lo = halves(b)
+    mul = functools.partial(jnp.dot, preferred_element_type=jnp.float32)
+    return mul(a_hi, b_hi) + (mul(a_hi, b_lo) + mul(a_lo, b_hi))
+
+
+def cells(tile, x):
+    return tile[:, x * WY:(x + 1) * WY]
+
+
+def speeds(vel):
+    u_pos = [-time_step * jnp.maximum(vel[0, x:x + 1, :], 0.0) for x in range(WX)]
+    u_neg = [-time_step * jnp.minimum(vel[0, x:x + 1, :], 0.0) for x in range(WX)]
+    return u_pos, u_neg
+
+
+def edges(u_pos, u_neg, lo2, lo1, hi0, hi1):
+    return ((-2.0 * u_pos[0]) * lo1 + (0.5 * u_pos[0]) * lo2,
+            (0.5 * u_pos[1]) * lo1,
+            (-0.5 * u_neg[2]) * hi0,
+            (2.0 * u_neg[3]) * hi0 + (-0.5 * u_neg[3]) * hi1)
+
+
+def rim_terms(vel, recv_lo, recv_hi, p):
+    lo2, lo1 = (recv_lo[pl.ds(p * 200 + j, QR, stride=2), :] for j in range(2))
+    hi0, hi1 = (recv_hi[pl.ds(p * 200 + j, QR, stride=2), :] for j in range(2))
+    return edges(*speeds(vel), lo2, lo1, hi0, hi1)
+
+
+def kernel(nx, ny, dens_hbm, vel_hbm, shear_hbm, herm_hbm, lag_hbm, ff_hbm, fs_hbm, sw_hbm,
+           acc, recv_lo, recv_hi, part, part_other,
+           dens, other, vel, shear, herm, lag, ff, fs, sw_in, sw_rows, sw,
+           send_lo, send_hi, rim, rim_lo, rim_hi,
+           xs, w_hi, w_lo, kqr_hi, kqr_lo, mom, mom_lo, mom_hi,
+           load_sem, in_sem, xs_send, xs_recv, col_sem, z_send, z_recv, m_send, m_recv, s_sem):
     gx, gy, col = lax.axis_index("gx"), lax.axis_index("gy"), lax.axis_index("col")
     x_next, x_prev = lax.rem(gx + 1, nx), lax.rem(gx + nx - 1, nx)
     y_next, y_prev = lax.rem(gy + 1, ny), lax.rem(gy + ny - 1, ny)
@@ -51,7 +89,10 @@
 
     loads = [pltpu.make_async_copy(dens_hbm.at[pl.ds(p * 400, 400)], dens.at[pl.ds(p * 400, 400)],
                                    load_sem.at[p]) for p in range(P_HERE)]
-    for c in loads:
+    smalls = [pltpu.make_async_copy(src, dst, in_sem.at[i]) for i, (src, dst) in enumerate((
+        (vel_hbm, vel), (herm_hbm, herm), (lag_hbm, lag), (sw_hbm, sw_in),
+        (ff_hbm, ff), (fs_hbm, fs), (shear_hbm, shear)))]
+    for c in loads + smalls:
         c.start()
     barrier = pltpu.get_barrier_semaphore()
     for d in (to_next, to_prev, to_up, to_down, to_col):
@@ -101,27 +142,36 @@
     for c in z_copies:
         c.start()
 
+    for c in smalls:
+        c.wait()
+    sw_rows[...] = jnp.zeros_like(sw_rows)
+    for p in range(P_HERE):
+        for q in range(HM):
+            at = (p * HM + q) * 8
+            sw_rows[at:at + 3, :] = sw_in[p, q]
+    lane_qr = iota((8, QR), 1)
+    q_of, r_hot = tenth(lane_qr), iota((HM, QR), 1)
+    spread = dot(sw_rows[...], one(r_hot - 10 * tenth(r_hot) == iota((HM, QR), 0)))
+    for p in range(P_HERE):
+        sw[p] = sum(jnp.where(q_of == q, spread[(p * HM + q) * 8:(p * HM + q) * 8 + 8], 0.0) for q in range(HM))
+
     row, hot = iota((QR, HM), 0), iota((QR, HM), 1)
     row_t, hot_t = iota((HM, QR), 1), iota((HM, QR), 0)
     rr, cc = iota((QR, QR), 0), iota((QR, QR), 1)
     rq, cq = tenth(rr), tenth(cc)
     h_exp = dot(dot(one(tenth(row) == hot), herm[...]), one(tenth(row_t) == hot_t))
     l_exp = dot(dot(one(row - 10 * tenth(row) == hot), lag[...]), one(row_t - 10 * tenth(row_t) == hot_t))
-    kqr[...] = time_step * (jnp.where(rr - 10 * rq == cc - 10 * cq, h_exp, 0.0) + jnp.where(rq == cq, l_exp, 0.0))
-
-    def cells(tile, x):
-        return tile[:, x * WY:(x + 1) * WY]
-
-    u_pos = [-time_step * jnp.maximum(vel[0, x:x + 1, :], 0.0) for x in range(WX)]
-    u_neg = [-time_step * jnp.minimum(vel[0, x:x + 1, :], 0.0) for x in range(WX)]
+    kqr_hi[...], kqr_lo[...] = halves(time_step * (jnp.where(rr - 10 * rq == cc - 10 * cq, h_exp, 0.0) + jnp.where(rq == cq, l_exp, 0.0)))
+
+    u_pos, u_neg = speeds(vel)
 
     mom[...] = jnp.zeros_like(mom)
 
     def own(p, _):
         c = [dens[pl.ds(p * 400 + x, QR, stride=WX), :] for x in range(WX)]
         block = jnp.concatenate(c, axis=1)
-        rate = dot(kqr[...], block)
-        mom[0:3, :] += dot(sw[p], block)
+        rate = dot3(kqr_hi[...], kqr_lo[...], block)
+        mom[...] += dot(sw[p], block)
         for x in range(WX):
             value = cells(rate, x) + (1.5 * (u_pos[x] - u_neg[x])) * c[x]
             if x >= 1:
@@ -143,22 +193,23 @@
             c.start()
 
     my0, other0 = col * P_HERE, (1 - col) * P_HERE
-    r1, k1 = iota((PQ, 40), 0), iota((PQ, 40), 1)
-    r1h, k1h = iota((PQ, HM), 0), iota((PQ, HM), 1)
+    r1, k1 = iota((WR, 50), 0), iota((WR, 50), 1)
+    comp = sum(jnp.where(r1 >= PQ * c, 1, 0) for c in range(1, 5))
+    r1 = jnp.where(r1 < 5 * PQ, r1 - PQ * comp, PQ)
+    flow, a_of = comp < 4, tenth(r1)
+    b_of = r1 - 10 * a_of
+    a_hot = one((r1 < 50) & (k1 == jnp.where(flow, 4 * (my0 + a_of) + comp, 40 + my0 + a_of)))
+    b_hot = one((r1 < 50) & (k1 == jnp.where(flow, 4 * b_of + comp, 40 + b_of)))
     c2, j2 = iota((HM, 2 * PQ), 1), iota((HM, 2 * PQ), 0)
     near = c2 < PQ
     c2 = jnp.where(near, c2, c2 - PQ)
     real = c2 < 50
     p_hot = one(real & (j2 == jnp.where(near, my0, other0) + tenth(c2)))
     q_hot = one(real & (j2 == c2 - 10 * tenth(c2)))
-    b_hot = one((r1h < 50) & (k1h == r1h - 10 * tenth(r1h)))
-    a_hot = one((r1h < 50) & (k1h == my0 + tenth(r1h)))
-    wmat[0:PQ, :] = time_step * dot(dot(a_hot, herm[...]), p_hot) * dot(b_hot, q_hot)
-    for c in range(4):
-        a_c = one((r1 < 50) & (k1 == 4 * (my0 + tenth(r1)) + c))
-        b_c = one((r1 < 50) & (k1 == 4 * (r1 - 10 * tenth(r1)) + c))
-        wmat[(c + 1) * PQ:(c + 2) * PQ, :] = time_step * (
-            dot(dot(a_c, ff[...]), p_hot) * dot(dot(b_c, fs[...]), q_hot))
+    eye = one(iota((HM, HM), 0) == iota((HM, HM), 1))
+    first = dot(dot(a_hot, jnp.concatenate([ff[...], herm[...]], axis=0)), p_hot)
+    second = dot(dot(b_hot, jnp.concatenate([fs[...], eye], axis=0)), q_hot)
+    w_hi[...], w_lo[...] = halves(time_step * first * second)
     xs[...] = jnp.zeros_like(xs)
 
     for c in z_copies:
@@ -194,11 +245,11 @@
             rows = pl.ds(r * WX + x, 50, stride=40)
             xs[0:50, x * WY:(x + 1) * WY] = dens[rows, :]
             xs[PQ:PQ + 50, x * WY:(x + 1) * WY] = other[rows, :]
-        t = dot(wmat[...], xs[...])
+        t = dot3(w_hi[...], w_lo[...], xs[...])
         for x in range(WX):
-            value = cells(t, x)[0:50]
+            value = cells(t, x)[4 * PQ:4 * PQ + 50]
             for c in range(4):
-                value += shear[c, x:x + 1, :] * cells(t, x)[(c + 1) * PQ:(c + 1) * PQ + 50]
+                value += shear[c, x:x + 1, :] * cells(t, x)[c * PQ:c * PQ + 50]
             acc[pl.ds(r * WX + x, 50, stride=40), :] += value
         return 0
 
@@ -208,78 +259,94 @@
 
     def moments(p, _):
         block = jnp.concatenate([acc[pl.ds(p * 400 + x, QR, stride=WX), :] for x in range(WX)], axis=1)
-        part[0:3, :] += dot(sw[p], block)
+        part[...] += dot(sw[p], block)
         return 0
 
     lax.fori_loop(0, P_HERE, moments, 0)
     for c in m_copies:
         c.wait_recv()
 
-    def edges(lo2, lo1, hi0, hi1):
-        return ((-2.0 * u_pos[0]) * lo1 + (0.5 * u_pos[0]) * lo2,
-                (0.5 * u_pos[1]) * lo1,
-                (-0.5 * u_neg[2]) * hi0,
-                (2.0 * u_neg[3]) * hi0 + (-0.5 * u_neg[3]) * hi1)
-
-    rims = edges(cells(mom_lo, 2), cells(mom_lo, 3), cells(mom_hi, 0), cells(mom_hi, 1))
+    rims = edges(u_pos, u_neg, cells(mom_lo, 2), cells(mom_lo, 3), cells(mom_hi, 0), cells(mom_hi, 1))
     for x in range(WX):
         part[:, x * WY:(x + 1) * WY] += rims[x]
     s_copy.start()
 
-    outs = []
     for p in range(P_HERE):
         for c in x_copies[p]:
             c.wait_recv()
-        lo2, lo1 = (recv_lo[pl.ds(p * 200 + j, QR, stride=2), :] for j in range(2))
-        hi0, hi1 = (recv_hi[pl.ds(p * 200 + j, QR, stride=2), :] for j in range(2))
-        add = edges(lo2, lo1, hi0, hi1)
-        for x in range(WX):
-            acc[pl.ds(p * 400 + x, QR, stride=WX), :] += add[x]
-        out = pltpu.make_async_copy(acc.at[pl.ds(p * 400, 400)], out_hbm.at[pl.ds(p * 400, 400)], out_sem.at[p])
-        out.start()
-        outs.append(out)
+        if p < LAST:
+            add = rim_terms(vel, recv_lo, recv_hi, p)
+            for x in range(WX):
+                acc[pl.ds(p * 400 + x, QR, stride=WX), :] += add[x]
     s_copy.wait_recv()
+    for pair in x_copies + [z_copies, m_copies, (col_copy, s_copy)]:
+        for c in pair:
+            c.wait_send()
+
+
+def finish(acc, recv_lo, recv_hi, part, part_other, vel, out_hbm, stress_out, last, sem):
+    outs = [pltpu.make_async_copy(acc.at[pl.ds(p * 400, 400)], out_hbm.at[pl.ds(p * 400, 400)], sem.at[p])
+            for p in range(LAST)]
+    outs.append(pltpu.make_async_copy(last, out_hbm.at[pl.ds(LAST * 400, 400)], sem.at[LAST]))
+    for c in outs[:LAST]:
+        c.start()
+    add = rim_terms(vel, recv_lo, recv_hi, LAST)
+    for x in range(WX):
+        last[pl.ds(x, QR, stride=WX), :] = acc[pl.ds(LAST * 400 + x, QR, stride=WX), :] + add[x]
+    outs[LAST].start()
     total = part[...] + part_other[...]
     for x in range(WX):
         stress_out[:, x, :] = cells(total, x)[0:3]
-    for pair in x_copies + [z_copies, m_copies, (col_copy, s_copy)]:
-        for c in pair:
-            c.wait_send()
-    for out in outs:
-        out.wait()
+    for c in outs:
+        c.wait()
 
 
 def body(nx, ny, density, velocity, shear_rates, hermite_matrix, laguerre_matrix, flow_first,
          flow_second, stress_weights):
     assert density.shape == (P_HERE, HM, HM, WX, WY)
-    f32 = jnp.float32
+    f32, bf16 = jnp.float32, jnp.bfloat16
     vmem = pl.BlockSpec(memory_space=pltpu.VMEM)
-    hbm = pl.BlockSpec(memory_space=pl.ANY)
+    hbm = pl.BlockSpec(memory_space=pltpu.HBM)
     dma = pltpu.SemaphoreType.DMA
-    advanced, stress = pl.pallas_call(
+    whole, half = (ROWS, WY), (ROWS // 2, WY)
+    rims, sums = (8 * GROUPS, WY), (8, WX * WY)
+    flows = (4 * HM, HM)
+    acc, recv_lo, recv_hi, part, part_other = pl.pallas_call(
         functools.partial(kernel, nx, ny),
-        out_shape=(jax.ShapeDtypeStruct((ROWS, WY), f32), jax.ShapeDtypeStruct((3, WX, WY), f32)),
-        in_specs=[hbm] + [vmem] * 7,
-        out_specs=(hbm, vmem),
+        out_shape=[jax.ShapeDtypeStruct(s, f32) for s in (whole, half, half, sums, sums)],
+        in_specs=[hbm] * 8,
+        out_specs=[vmem] * 5,
         scratch_shapes=[
-            pltpu.VMEM((ROWS, WY), f32), pltpu.VMEM((ROWS, WY), f32), pltpu.VMEM((ROWS, WY), f32),
-            pltpu.VMEM((ROWS // 2, WY), f32), pltpu.VMEM((ROWS // 2, WY), f32),
-            pltpu.VMEM((ROWS // 2, WY), f32), pltpu.VMEM((ROWS // 2, WY), f32),
-            pltpu.VMEM((8 * GROUPS, WY), f32), pltpu.VMEM((8 * GROUPS, WY), f32), pltpu.VMEM((8 * GROUPS, WY), f32),
-            pltpu.VMEM((2 * PQ, WX * WY), f32), pltpu.VMEM((5 * PQ, 2 * PQ), f32), pltpu.VMEM((QR, QR), f32),
-            pltpu.VMEM((8, WX * WY), f32), pltpu.VMEM((8, WX * WY), f32), pltpu.VMEM((8, WX * WY), f32),
-            pltpu.VMEM((8, WX * WY), f32), pltpu.VMEM((8, WX * WY), f32),
-            dma((P_HERE,)), dma((P_HERE,)), dma((2, P_HERE)), dma((2, P_HERE)), dma((2,)),
+            pltpu.VMEM(whole, f32), pltpu.VMEM(whole, f32),
+            pltpu.VMEM((2, WX, WY), f32), pltpu.VMEM((4, WX, WY), f32),
+            pltpu.VMEM((HM, HM), f32), pltpu.VMEM((HM, HM), f32),
+            pltpu.VMEM(flows, f32), pltpu.VMEM(flows, f32),
+            pltpu.VMEM((P_HERE, HM, 3, HM), f32), pltpu.VMEM((P_HERE * HM * 8, HM), f32),
+            pltpu.VMEM((P_HERE, 8, QR), f32),
+            pltpu.VMEM(half, f32), pltpu.VMEM(half, f32),
+            pltpu.VMEM(rims, f32), pltpu.VMEM(rims, f32), pltpu.VMEM(rims, f32),
+            pltpu.VMEM((2 * PQ, WX * WY), f32), pltpu.VMEM((WR, 2 * PQ), bf16), pltpu.VMEM((WR, 2 * PQ), bf16),
+            pltpu.VMEM((QR, QR), bf16), pltpu.VMEM((QR, QR), bf16),
+            pltpu.VMEM(sums, f32), pltpu.VMEM(sums, f32), pltpu.VMEM(sums, f32),
+            dma((P_HERE,)), dma((7,)), dma((2, P_HERE)), dma((2, P_HERE)), dma((2,)),
             dma((2,)), dma((2,)), dma((2,)), dma((2,)), dma((2,)),
         ],
         compiler_params=pltpu.CompilerParams(collective_id=0, has_side_effects=True,
-                                             vmem_limit_bytes=32 * 1024 * 1024),
+                                             vmem_limit_bytes=52700 * 1024),
         cost_estimate=pl.CostEstimate(flops=600_000_000, bytes_accessed=3_000_000, transcendentals=0),
     )(
-        density.reshape(ROWS, WY), velocity, shear_rates, hermite_matrix, laguerre_matrix,
-        flow_first.transpose(1, 0, 2).reshape(4 * HM, HM), flow_second.transpose(1, 0, 2).reshape(4 * HM, HM),
-        stress_weights.reshape(3, P_HERE, QR).transpose(1, 0, 2),
+        density.reshape(whole), velocity, shear_rates, hermite_matrix, laguerre_matrix,
+        flow_first.transpose(1, 0, 2).reshape(flows), flow_second.transpose(1, 0, 2).reshape(flows),
+        stress_weights.transpose(1, 2, 0, 3),
     )
+    advanced, stress = pl.pallas_call(
+        finish,
+        out_shape=(jax.ShapeDtypeStruct(whole, f32), jax.ShapeDtypeStruct((3, WX, WY), f32)),
+        in_specs=[vmem] * 6,
+        out_specs=(hbm, vmem),
+        scratch_shapes=[pltpu.VMEM((QR * WX, WY), f32), dma((P_HERE,))],
+        cost_estimate=pl.CostEstimate(flops=1_000_000, bytes_accessed=2_000_000, transcendentals=0),
+    )(acc, recv_lo, recv_hi, part, part_other, velocity)
     return advanced.reshape(density.shape), stress
 
 

time: 37 us -> 43.2 us (1.17)
  local copies, waits for them, and re-layouts: 4.4 us -> 8.89 us
  Pallas kernels: 31.7 us -> 33.2 us
    unnamed x17 -> x24, local copies, waits for them, and re-layouts: 4.3 us -> 8.89 us
    pallas_call x1 -> x2, Pallas kernels: 31.7 us -> 33.2 us  [the longest x1 30.1 us: body(): pl.pallas_call(functools.partial(kernel, nx, ny), out_shape=[jax.ShapeDty...]
where the time goes in v1:
time: 43.2 us; the launch traced here: 42.8 us
  Pallas kernels  33.2 us (77%)
  local copies, waits for them, and re-layouts  8.89 us (21%)
  between operations  0.67 us (2%)
    pallas_call x1, Pallas kernels, body(): pl.pallas_call(functools.partial(kernel, nx, ny), out_shape=[jax.ShapeDty...  30.1 us
    unnamed x24, local copies, waits for them, and re-layouts  8.89 us
    pallas_call x1, Pallas kernels, body(): pl.pallas_call(finish, out_shape=(jax.ShapeDtypeStruct(whole, f32), jax.S...  3.11 us

profile of v1, /device:TPU:0, one launch (start us, length us, event | category | flops | bytes accessed | tf_op | source)
XLA Modules:
  0.0 42.8 jit_solution(3283558935529084442)
XLA Ops:
  0.6 0.0 copy-start.5
  0.6 0.7 %copy-done.5 = f32[2,4,128]{2,1,0:T(4,128)S(1)} copy-done((f32[2,4,128]{2,1,0:T(4,128)S(1)}, f32[2,4,128]{2,1,0:T(4,128)}, u32[]{:S(2)}) %copy-start.5) | copy-done | bytes 4120
  1.3 0.0 copy-start.6
  1.3 0.9 %copy-done.6 = f32[3,5,10,10]{3,0,2,1:T(4,128)S(1)} copy-done((f32[3,5,10,10]{3,0,2,1:T(4,128)S(1)}, f32[3,5,10,10]{3,0,2,1:T(4,128)}, u32[]{:S(2)}) %copy-start.6) | copy-done | bytes 6024
  2.2 0.0 copy-start.7
  2.2 0.7 %copy-done.7 = f32[4,10,10]{2,0,1:T(4,128)S(1)} copy-done((f32[4,10,10]{2,0,1:T(4,128)S(1)}, f32[4,10,10]{2,0,1:T(4,128)}, u32[]{:S(2)}) %copy-start.7) | copy-done | bytes 1624
  2.9 0.0 copy-start.8
  2.9 0.7 %copy-done.8 = f32[4,10,10]{2,0,1:T(4,128)S(1)} copy-done((f32[4,10,10]{2,0,1:T(4,128)S(1)}, f32[4,10,10]{2,0,1:T(4,128)}, u32[]{:S(2)}) %copy-start.8) | copy-done | bytes 1624
  3.7 0.0 copy-start.9
  3.7 0.7 %copy-done.9 = f32[4,4,128]{2,1,0:T(4,128)S(1)} copy-done((f32[4,4,128]{2,1,0:T(4,128)S(1)}, f32[4,4,128]{2,1,0:T(4,128)}, u32[]{:S(2)}) %copy-start.9) | copy-done | bytes 8216
  4.4 0.0 copy-start.10
  4.4 0.7 %copy-done.10 = f32[10,10]{1,0:T(8,128)S(1)} copy-done((f32[10,10]{1,0:T(8,128)S(1)}, f32[10,10]{1,0:T(8,128)}, u32[]{:S(2)}) %copy-start.10) | copy-done | bytes 424
  5.1 0.0 copy-start.11
  5.1 0.7 %copy-done.11 = f32[10,10]{1,0:T(8,128)S(1)} copy-done((f32[10,10]{1,0:T(8,128)S(1)}, f32[10,10]{1,0:T(8,128)}, u32[]{:S(2)}) %copy-start.11) | copy-done | bytes 424
  5.8 30.1 %shard_map.95 = (f32[2000,128]{1,0:T(8,128)S(1)}, f32[1000,128]{1,0:T(8,128)S(1)}, f32[1000,128]{1,0:T(8,128)S(1)}, f32[8,512]{1,0:T(8,128)S(1)}, f32[8,512]{1,0:T(8,128)S(1)}) custom-call(f32[2000,128]{1,0:T(8,128)} %bitcast.12, f32[2,4,128]{2,1,0:T(4,128)S(1)} %copy-done.5, f32[4,4,128]{2,1,0:T(4,128)S(1)} %copy-done.9, f32[10,10]{1,0:T(8,128)S(1)} %copy-done.10, ...), custom_call_target="tpu_custom_call" | custom-call | flops 600000000 | bytes 3000000 | tf_op jit(solution)/shard_map/pallas_call | solution.py:314
  35.9 0.0 copy-start
  35.9 1.0 %copy-done = f32[2000,128]{1,0:T(8,128)} copy-done((f32[2000,128]{1,0:T(8,128)}, f32[2000,128]{1,0:T(8,128)S(1)}, u32[]{:S(2)}) %copy-start) | copy-done | bytes 1024024
  36.9 0.0 copy-start.1
  36.9 0.8 %copy-done.1 = f32[1000,128]{1,0:T(8,128)} copy-done((f32[1000,128]{1,0:T(8,128)}, f32[1000,128]{1,0:T(8,128)S(1)}, u32[]{:S(2)}) %copy-start.1) | copy-done | bytes 512024
  37.7 0.0 copy-start.2
  37.7 0.8 %copy-done.2 = f32[1000,128]{1,0:T(8,128)} copy-done((f32[1000,128]{1,0:T(8,128)}, f32[1000,128]{1,0:T(8,128)S(1)}, u32[]{:S(2)}) %copy-start.2) | copy-done | bytes 512024
  38.5 0.0 copy-start.3
  38.5 0.6 %copy-done.3 = f32[8,512]{1,0:T(8,128)} copy-done((f32[8,512]{1,0:T(8,128)}, f32[8,512]{1,0:T(8,128)S(1)}, u32[]{:S(2)}) %copy-start.3) | copy-done | bytes 16408
  39.1 0.0 copy-start.4
  39.1 0.6 %copy-done.4 = f32[8,512]{1,0:T(8,128)} copy-done((f32[8,512]{1,0:T(8,128)}, f32[8,512]{1,0:T(8,128)S(1)}, u32[]{:S(2)}) %copy-start.4) | copy-done | bytes 16408
  39.7 3.1 %shard_map.96 = (f32[2000,128]{1,0:T(8,128)}, f32[3,4,128]{2,1,0:T(4,128)}) custom-call(f32[2000,128]{1,0:T(8,128)} %copy-done, f32[1000,128]{1,0:T(8,128)} %copy-done.1, f32[1000,128]{1,0:T(8,128)} %copy-done.2, f32[8,512]{1,0:T(8,128)} %copy-done.3, f32[8,512]{1,0:T(8,128)} %copy-done.4, f32[2,4,128]{2,1,0:T(4,128)} %vel.1), custom_call_target="tpu_custom_call" | custom-call | flops 1000000 | bytes 2000000 | tf_op jit(solution)/shard_map/pallas_call | solution.py:342
Async XLA Ops:
  0.6 0.7 %copy-start.5 = (f32[2,4,128]{2,1,0:T(4,128)S(1)}, f32[2,4,128]{2,1,0:T(4,128)}, u32[]{:S(2)}) copy-start(f32[2,4,128]{2,1,0:T(4,128)} %vel.1) | copy-start | bytes 12292
  1.3 0.9 %copy-start.6 = (f32[3,5,10,10]{3,0,2,1:T(4,128)S(1)}, f32[3,5,10,10]{3,0,2,1:T(4,128)}, u32[]{:S(2)}) copy-start(f32[3,5,10,10]{3,0,2,1:T(4,128)} %param.15) | copy-start | bytes 18004
  2.2 0.7 %copy-start.7 = (f32[4,10,10]{2,0,1:T(4,128)S(1)}, f32[4,10,10]{2,0,1:T(4,128)}, u32[]{:S(2)}) copy-start(f32[4,10,10]{2,0,1:T(4,128)} %param.13) | copy-start | bytes 4804
  2.9 0.7 %copy-start.8 = (f32[4,10,10]{2,0,1:T(4,128)S(1)}, f32[4,10,10]{2,0,1:T(4,128)}, u32[]{:S(2)}) copy-start(f32[4,10,10]{2,0,1:T(4,128)} %param.14) | copy-start | bytes 4804
  3.7 0.7 %copy-start.9 = (f32[4,4,128]{2,1,0:T(4,128)S(1)}, f32[4,4,128]{2,1,0:T(4,128)}, u32[]{:S(2)}) copy-start(f32[4,4,128]{2,1,0:T(4,128)} %shear_hbm.1) | copy-start | bytes 24580
  4.4 0.7 %copy-start.10 = (f32[10,10]{1,0:T(8,128)S(1)}, f32[10,10]{1,0:T(8,128)}, u32[]{:S(2)}) copy-start(f32[10,10]{1,0:T(8,128)} %herm_hbm.1) | copy-start | bytes 1204
  5.1 0.7 %copy-start.11 = (f32[10,10]{1,0:T(8,128)S(1)}, f32[10,10]{1,0:T(8,128)}, u32[]{:S(2)}) copy-start(f32[10,10]{1,0:T(8,128)} %lag_hbm.1) | copy-start | bytes 1204
  35.9 1.0 %copy-start = (f32[2000,128]{1,0:T(8,128)}, f32[2000,128]{1,0:T(8,128)S(1)}, u32[]{:S(2)}) copy-start(f32[2000,128]{1,0:T(8,128)S(1)} %get-tuple-element.9.acc) | copy-start | bytes 3072004
  36.9 0.8 %copy-start.1 = (f32[1000,128]{1,0:T(8,128)}, f32[1000,128]{1,0:T(8,128)S(1)}, u32[]{:S(2)}) copy-start(f32[1000,128]{1,0:T(8,128)S(1)} %get-tuple-element.10.recv_lo) | copy-start | bytes 1536004
  37.7 0.8 %copy-start.2 = (f32[1000,128]{1,0:T(8,128)}, f32[1000,128]{1,0:T(8,128)S(1)}, u32[]{:S(2)}) copy-start(f32[1000,128]{1,0:T(8,128)S(1)} %get-tuple-element.11.recv_hi) | copy-start | bytes 1536004
  38.5 0.6 %copy-start.3 = (f32[8,512]{1,0:T(8,128)}, f32[8,512]{1,0:T(8,128)S(1)}, u32[]{:S(2)}) copy-start(f32[8,512]{1,0:T(8,128)S(1)} %get-tuple-element.12.part) | copy-start | bytes 49156
  39.1 0.6 %copy-start.4 = (f32[8,512]{1,0:T(8,128)}, f32[8,512]{1,0:T(8,128)S(1)}, u32[]{:S(2)}) copy-start(f32[8,512]{1,0:T(8,128)S(1)} %get-tuple-element.13.part_other) | copy-start | bytes 49156

commit v2 on v1

--- a/solution.py
+++ b/solution.py
@@ -75,11 +75,11 @@
 
 
 def kernel(nx, ny, dens_hbm, vel_hbm, shear_hbm, herm_hbm, lag_hbm, ff_hbm, fs_hbm, sw_hbm,
-           acc, recv_lo, recv_hi, part, part_other,
-           dens, other, vel, shear, herm, lag, ff, fs, sw_in, sw_rows, sw,
+           out_hbm, stress_hbm,
+           acc, recv_lo, recv_hi, part, part_other, stress, dens, other, vel, shear, herm, lag, ff, fs, sw_in, sw_rows, sw,
            send_lo, send_hi, rim, rim_lo, rim_hi,
            xs, w_hi, w_lo, kqr_hi, kqr_lo, mom, mom_lo, mom_hi,
-           load_sem, in_sem, xs_send, xs_recv, col_sem, z_send, z_recv, m_send, m_recv, s_sem):
+           load_sem, in_sem, out_sem, xs_send, xs_recv, col_sem, z_send, z_recv, m_send, m_recv, s_sem):
     gx, gy, col = lax.axis_index("gx"), lax.axis_index("gy"), lax.axis_index("col")
     x_next, x_prev = lax.rem(gx + 1, nx), lax.rem(gx + nx - 1, nx)
     y_next, y_prev = lax.rem(gy + 1, ny), lax.rem(gy + ny - 1, ny)
@@ -271,33 +271,36 @@
         part[:, x * WY:(x + 1) * WY] += rims[x]
     s_copy.start()
 
-    for p in range(P_HERE):
+    outs = [pltpu.make_async_copy(acc.at[pl.ds(p * 400, 400)], out_hbm.at[pl.ds(p * 400, 400)], out_sem.at[p])
+            for p in range(P_HERE)]
+    outs.append(pltpu.make_async_copy(stress, stress_hbm, out_sem.at[P_HERE]))
+    for p in range(P_HERE):
+        if p == LAST:
+            s_copy.wait_recv()
+            total = part[...] + part_other[...]
+            for x in range(WX):
+                stress[:, x, :] = cells(total, x)[0:3]
+            outs[P_HERE].start()
         for c in x_copies[p]:
             c.wait_recv()
-        if p < LAST:
-            add = rim_terms(vel, recv_lo, recv_hi, p)
-            for x in range(WX):
-                acc[pl.ds(p * 400 + x, QR, stride=WX), :] += add[x]
-    s_copy.wait_recv()
+        add = rim_terms(vel, recv_lo, recv_hi, p)
+        for x in range(WX):
+            acc[pl.ds(p * 400 + x, QR, stride=WX), :] += add[x]
+        outs[p].start()
     for pair in x_copies + [z_copies, m_copies, (col_copy, s_copy)]:
         for c in pair:
             c.wait_send()
-
-
-def finish(acc, recv_lo, recv_hi, part, part_other, vel, out_hbm, stress_out, last, sem):
-    outs = [pltpu.make_async_copy(acc.at[pl.ds(p * 400, 400)], out_hbm.at[pl.ds(p * 400, 400)], sem.at[p])
-            for p in range(LAST)]
-    outs.append(pltpu.make_async_copy(last, out_hbm.at[pl.ds(LAST * 400, 400)], sem.at[LAST]))
-    for c in outs[:LAST]:
+    for c in outs:
+        c.wait()
+
+
+def hand_on(made, made_stress, out, stress, sem):
+    copies = [pltpu.make_async_copy(made.at[pl.ds(p * 400, 400)], out.at[pl.ds(p * 400, 400)], sem.at[p])
+              for p in range(P_HERE)]
+    copies.append(pltpu.make_async_copy(made_stress, stress, sem.at[P_HERE]))
+    for c in copies:
         c.start()
-    add = rim_terms(vel, recv_lo, recv_hi, LAST)
-    for x in range(WX):
-        last[pl.ds(x, QR, stride=WX), :] = acc[pl.ds(LAST * 400 + x, QR, stride=WX), :] + add[x]
-    outs[LAST].start()
-    total = part[...] + part_other[...]
-    for x in range(WX):
-        stress_out[:, x, :] = cells(total, x)[0:3]
-    for c in outs:
+    for c in copies:
         c.wait()
 
 
@@ -305,18 +308,21 @@
          flow_second, stress_weights):
     assert density.shape == (P_HERE, HM, HM, WX, WY)
     f32, bf16 = jnp.float32, jnp.bfloat16
-    vmem = pl.BlockSpec(memory_space=pltpu.VMEM)
     hbm = pl.BlockSpec(memory_space=pltpu.HBM)
     dma = pltpu.SemaphoreType.DMA
     whole, half = (ROWS, WY), (ROWS // 2, WY)
     rims, sums = (8 * GROUPS, WY), (8, WX * WY)
     flows = (4 * HM, HM)
-    acc, recv_lo, recv_hi, part, part_other = pl.pallas_call(
+    results = (jax.ShapeDtypeStruct(whole, f32), jax.ShapeDtypeStruct((3, WX, WY), f32))
+    params = functools.partial(pltpu.CompilerParams, vmem_limit_bytes=60 * 1024 * 1024)
+    made = pl.pallas_call(
         functools.partial(kernel, nx, ny),
-        out_shape=[jax.ShapeDtypeStruct(s, f32) for s in (whole, half, half, sums, sums)],
+        out_shape=results,
         in_specs=[hbm] * 8,
-        out_specs=[vmem] * 5,
+        out_specs=(hbm, hbm),
         scratch_shapes=[
+            pltpu.VMEM(whole, f32), pltpu.VMEM(half, f32), pltpu.VMEM(half, f32),
+            pltpu.VMEM(sums, f32), pltpu.VMEM(sums, f32), pltpu.VMEM((3, WX, WY), f32),
             pltpu.VMEM(whole, f32), pltpu.VMEM(whole, f32),
             pltpu.VMEM((2, WX, WY), f32), pltpu.VMEM((4, WX, WY), f32),
             pltpu.VMEM((HM, HM), f32), pltpu.VMEM((HM, HM), f32),
@@ -328,11 +334,10 @@
             pltpu.VMEM((2 * PQ, WX * WY), f32), pltpu.VMEM((WR, 2 * PQ), bf16), pltpu.VMEM((WR, 2 * PQ), bf16),
             pltpu.VMEM((QR, QR), bf16), pltpu.VMEM((QR, QR), bf16),
             pltpu.VMEM(sums, f32), pltpu.VMEM(sums, f32), pltpu.VMEM(sums, f32),
-            dma((P_HERE,)), dma((7,)), dma((2, P_HERE)), dma((2, P_HERE)), dma((2,)),
+            dma((P_HERE,)), dma((7,)), dma((P_HERE + 1,)), dma((2, P_HERE)), dma((2, P_HERE)), dma((2,)),
             dma((2,)), dma((2,)), dma((2,)), dma((2,)), dma((2,)),
         ],
-        compiler_params=pltpu.CompilerParams(collective_id=0, has_side_effects=True,
-                                             vmem_limit_bytes=52700 * 1024),
+        compiler_params=params(collective_id=0, has_side_effects=True),
         cost_estimate=pl.CostEstimate(flops=600_000_000, bytes_accessed=3_000_000, transcendentals=0),
     )(
         density.reshape(whole), velocity, shear_rates, hermite_matrix, laguerre_matrix,
@@ -340,13 +345,14 @@
         stress_weights.transpose(1, 2, 0, 3),
     )
     advanced, stress = pl.pallas_call(
-        finish,
-        out_shape=(jax.ShapeDtypeStruct(whole, f32), jax.ShapeDtypeStruct((3, WX, WY), f32)),
-        in_specs=[vmem] * 6,
-        out_specs=(hbm, vmem),
-        scratch_shapes=[pltpu.VMEM((QR * WX, WY), f32), dma((P_HERE,))],
-        cost_estimate=pl.CostEstimate(flops=1_000_000, bytes_accessed=2_000_000, transcendentals=0),
-    )(acc, recv_lo, recv_hi, part, part_other, velocity)
+        hand_on,
+        out_shape=results,
+        in_specs=[hbm, hbm],
+        out_specs=(hbm, hbm),
+        scratch_shapes=[dma((P_HERE + 1,))],
+        compiler_params=params(),
+        cost_estimate=pl.CostEstimate(flops=0, bytes_accessed=2_000_000, transcendentals=0),
+    )(*made)
     return advanced.reshape(density.shape), stress
 
 

time: 43.2 us -> 64 us (1.48)
  Pallas kernels: 33.2 us -> 63.2 us
  local copies, waits for them, and re-layouts: 8.89 us -> 0 us
    pallas_call x2, Pallas kernels: 33.2 us -> 63.2 us  [the longest x1 32.4 us: body(): pl.pallas_call(hand_on, out_shape=results, in_specs=[hbm, hbm], out_specs...]
    unnamed x24 -> x0, local copies, waits for them, and re-layouts: 8.89 us -> none
where the time goes in v2:
time: 64 us; the launch traced here: 63.8 us
  Pallas kernels  63.2 us (99%)
  between operations  0.64 us (1%)
    pallas_call x1, Pallas kernels, body(): pl.pallas_call(hand_on, out_shape=results, in_specs=[hbm, hbm], out_specs...  32.4 us
    pallas_call x1, Pallas kernels, body(): pl.pallas_call(functools.partial(kernel, nx, ny), out_shape=results, in_s...  30.8 us

profile of v2, /device:TPU:0, one launch (start us, length us, event | category | flops | bytes accessed | tf_op | source)
XLA Modules:
  0.0 63.8 jit_solution(5749492311012527715)
XLA Ops:
  0.6 30.8 %shard_map.95 = (f32[2000,128]{1,0:T(8,128)}, f32[3,4,128]{2,1,0:T(4,128)}) custom-call(f32[2000,128]{1,0:T(8,128)} %bitcast.9, f32[2,4,128]{2,1,0:T(4,128)} %vel_hbm.1, f32[4,4,128]{2,1,0:T(4,128)} %shear_hbm.1, f32[10,10]{1,0:T(8,128)} %herm_hbm.1, f32[10,10]{1,0:T(8,128)} %lag_hbm.1, f32[40,10]{1,0:T(8,128)} %bitcast.12, f32[40,10]{1,0:T(8,128)} %bitcast.13, ...), custom_call_target="tpu_custom_call" | custom-call | flops 600000000 | bytes 3000000 | tf_op jit(solution)/shard_map/pallas_call | solution.py:318
  31.5 32.4 %shard_map.96 = (f32[2000,128]{1,0:T(8,128)}, f32[3,4,128]{2,1,0:T(4,128)}) custom-call(f32[2000,128]{1,0:T(8,128)} %get-tuple-element.6.made, f32[3,4,128]{2,1,0:T(4,128)} %get-tuple-element.7.made_stress), custom_call_target="tpu_custom_call" | custom-call | bytes 2000000 | tf_op jit(solution)/shard_map/pallas_call | solution.py:347

commit v3 on v2

--- a/solution.py
+++ b/solution.py
@@ -294,16 +294,6 @@
         c.wait()
 
 
-def hand_on(made, made_stress, out, stress, sem):
-    copies = [pltpu.make_async_copy(made.at[pl.ds(p * 400, 400)], out.at[pl.ds(p * 400, 400)], sem.at[p])
-              for p in range(P_HERE)]
-    copies.append(pltpu.make_async_copy(made_stress, stress, sem.at[P_HERE]))
-    for c in copies:
-        c.start()
-    for c in copies:
-        c.wait()
-
-
 def body(nx, ny, density, velocity, shear_rates, hermite_matrix, laguerre_matrix, flow_first,
          flow_second, stress_weights):
     assert density.shape == (P_HERE, HM, HM, WX, WY)
@@ -314,8 +304,7 @@
     rims, sums = (8 * GROUPS, WY), (8, WX * WY)
     flows = (4 * HM, HM)
     results = (jax.ShapeDtypeStruct(whole, f32), jax.ShapeDtypeStruct((3, WX, WY), f32))
-    params = functools.partial(pltpu.CompilerParams, vmem_limit_bytes=60 * 1024 * 1024)
-    made = pl.pallas_call(
+    advanced, stress = pl.pallas_call(
         functools.partial(kernel, nx, ny),
         out_shape=results,
         in_specs=[hbm] * 8,
@@ -337,22 +326,14 @@
             dma((P_HERE,)), dma((7,)), dma((P_HERE + 1,)), dma((2, P_HERE)), dma((2, P_HERE)), dma((2,)),
             dma((2,)), dma((2,)), dma((2,)), dma((2,)), dma((2,)),
         ],
-        compiler_params=params(collective_id=0, has_side_effects=True),
+        compiler_params=pltpu.CompilerParams(collective_id=0, has_side_effects=True,
+                                             vmem_limit_bytes=60 * 1024 * 1024),
         cost_estimate=pl.CostEstimate(flops=600_000_000, bytes_accessed=3_000_000, transcendentals=0),
     )(
         density.reshape(whole), velocity, shear_rates, hermite_matrix, laguerre_matrix,
         flow_first.transpose(1, 0, 2).reshape(flows), flow_second.transpose(1, 0, 2).reshape(flows),
         stress_weights.transpose(1, 2, 0, 3),
     )
-    advanced, stress = pl.pallas_call(
-        hand_on,
-        out_shape=results,
-        in_specs=[hbm, hbm],
-        out_specs=(hbm, hbm),
-        scratch_shapes=[dma((P_HERE + 1,))],
-        compiler_params=params(),
-        cost_estimate=pl.CostEstimate(flops=0, bytes_accessed=2_000_000, transcendentals=0),
-    )(*made)
     return advanced.reshape(density.shape), stress
 
 

time: 64 us -> 34.5 us (0.54)
  Pallas kernels: 63.2 us -> 30.8 us
  local copies, waits for them, and re-layouts: 0 us -> 2.84 us
    pallas_call x1 -> x0, Pallas kernels: 32.4 us -> none  [body(): pl.pallas_call(hand_on, out_shape=results, in_specs=[hbm, hbm], out_specs...]
    unnamed x0 -> x4, local copies, waits for them, and re-layouts: none -> 2.84 us
where the time goes in v3:
time: 34.5 us; the launch traced here: 34.3 us
  Pallas kernels  30.8 us (89%)
  local copies, waits for them, and re-layouts  2.84 us (8%)
  between operations  0.65 us (2%)
    pallas_call x1, Pallas kernels, body(): pl.pallas_call(functools.partial(kernel, nx, ny), out_shape=results, in_s...  30.8 us
    unnamed x4, local copies, waits for them, and re-layouts  2.84 us

profile of v3, /device:TPU:0, one launch (start us, length us, event | category | flops | bytes accessed | tf_op | source)
XLA Modules:
  0.0 34.3 jit_solution(7776338312781958630)
XLA Ops:
  0.6 30.8 %shard_map.95 = (f32[2000,128]{1,0:T(8,128)}, f32[3,4,128]{2,1,0:T(4,128)}) custom-call(f32[2000,128]{1,0:T(8,128)} %bitcast.10, f32[2,4,128]{2,1,0:T(4,128)} %vel_hbm.1, f32[4,4,128]{2,1,0:T(4,128)} %shear_hbm.1, f32[10,10]{1,0:T(8,128)} %herm_hbm.1, f32[10,10]{1,0:T(8,128)} %lag_hbm.1, f32[40,10]{1,0:T(8,128)} %bitcast.12, f32[40,10]{1,0:T(8,128)} %bitcast.13, ...), custom_call_target="tpu_custom_call" | custom-call | flops 600000000 | bytes 3000000 | tf_op jit(solution)/shard_map/pallas_call | solution.py:307
  31.5 0.0 copy-start
  31.5 2.2 %copy.12 = f32[5,10,10,4,128]{4,3,2,1,0:T(4,128)} copy(f32[5,10,10,4,128]{4,3,2,1,0:T(4,128)} %bitcast.9) | data formatting | bytes 2048000
  33.7 0.0 copy-done
  33.7 0.6 %copy.13 = f32[3,4,128]{2,1,0:T(4,128)} copy(f32[3,4,128]{2,1,0:T(4,128)S(1)} %copy-done) | data formatting | bytes 12288
Async XLA Ops:
  31.5 2.3 %copy-start = (f32[3,4,128]{2,1,0:T(4,128)S(1)}, f32[3,4,128]{2,1,0:T(4,128)}, u32[]{:S(2)}) copy-start(f32[3,4,128]{2,1,0:T(4,128)} %get-tuple-element.9) | copy-start | bytes 18436

commit v4 on v3

--- a/solution.py
+++ b/solution.py
@@ -75,11 +75,11 @@
 
 
 def kernel(nx, ny, dens_hbm, vel_hbm, shear_hbm, herm_hbm, lag_hbm, ff_hbm, fs_hbm, sw_hbm,
-           out_hbm, stress_hbm,
-           acc, recv_lo, recv_hi, part, part_other, stress, dens, other, vel, shear, herm, lag, ff, fs, sw_in, sw_rows, sw,
+           acc, stress,
+           recv_lo, recv_hi, part, part_other, dens, other, vel, shear, herm, lag, ff, fs, sw_in, sw_rows, sw,
            send_lo, send_hi, rim, rim_lo, rim_hi,
            xs, w_hi, w_lo, kqr_hi, kqr_lo, mom, mom_lo, mom_hi,
-           load_sem, in_sem, out_sem, xs_send, xs_recv, col_sem, z_send, z_recv, m_send, m_recv, s_sem):
+           load_sem, in_sem, xs_send, xs_recv, col_sem, z_send, z_recv, m_send, m_recv, s_sem):
     gx, gy, col = lax.axis_index("gx"), lax.axis_index("gy"), lax.axis_index("col")
     x_next, x_prev = lax.rem(gx + 1, nx), lax.rem(gx + nx - 1, nx)
     y_next, y_prev = lax.rem(gy + 1, ny), lax.rem(gy + ny - 1, ny)
@@ -271,27 +271,20 @@
         part[:, x * WY:(x + 1) * WY] += rims[x]
     s_copy.start()
 
-    outs = [pltpu.make_async_copy(acc.at[pl.ds(p * 400, 400)], out_hbm.at[pl.ds(p * 400, 400)], out_sem.at[p])
-            for p in range(P_HERE)]
-    outs.append(pltpu.make_async_copy(stress, stress_hbm, out_sem.at[P_HERE]))
     for p in range(P_HERE):
         if p == LAST:
             s_copy.wait_recv()
             total = part[...] + part_other[...]
             for x in range(WX):
                 stress[:, x, :] = cells(total, x)[0:3]
-            outs[P_HERE].start()
         for c in x_copies[p]:
             c.wait_recv()
         add = rim_terms(vel, recv_lo, recv_hi, p)
         for x in range(WX):
             acc[pl.ds(p * 400 + x, QR, stride=WX), :] += add[x]
-        outs[p].start()
     for pair in x_copies + [z_copies, m_copies, (col_copy, s_copy)]:
         for c in pair:
             c.wait_send()
-    for c in outs:
-        c.wait()
 
 
 def body(nx, ny, density, velocity, shear_rates, hermite_matrix, laguerre_matrix, flow_first,
@@ -299,19 +292,19 @@
     assert density.shape == (P_HERE, HM, HM, WX, WY)
     f32, bf16 = jnp.float32, jnp.bfloat16
     hbm = pl.BlockSpec(memory_space=pltpu.HBM)
+    vmem = pl.BlockSpec(memory_space=pltpu.VMEM)
     dma = pltpu.SemaphoreType.DMA
     whole, half = (ROWS, WY), (ROWS // 2, WY)
     rims, sums = (8 * GROUPS, WY), (8, WX * WY)
     flows = (4 * HM, HM)
-    results = (jax.ShapeDtypeStruct(whole, f32), jax.ShapeDtypeStruct((3, WX, WY), f32))
+    results = (pltpu.VMEM(whole, f32), pltpu.VMEM((3, WX, WY), f32))
     advanced, stress = pl.pallas_call(
         functools.partial(kernel, nx, ny),
         out_shape=results,
         in_specs=[hbm] * 8,
-        out_specs=(hbm, hbm),
+        out_specs=(vmem, vmem),
         scratch_shapes=[
-            pltpu.VMEM(whole, f32), pltpu.VMEM(half, f32), pltpu.VMEM(half, f32),
-            pltpu.VMEM(sums, f32), pltpu.VMEM(sums, f32), pltpu.VMEM((3, WX, WY), f32),
+            pltpu.VMEM(half, f32), pltpu.VMEM(half, f32), pltpu.VMEM(sums, f32), pltpu.VMEM(sums, f32),
             pltpu.VMEM(whole, f32), pltpu.VMEM(whole, f32),
             pltpu.VMEM((2, WX, WY), f32), pltpu.VMEM((4, WX, WY), f32),
             pltpu.VMEM((HM, HM), f32), pltpu.VMEM((HM, HM), f32),
@@ -323,17 +316,17 @@
             pltpu.VMEM((2 * PQ, WX * WY), f32), pltpu.VMEM((WR, 2 * PQ), bf16), pltpu.VMEM((WR, 2 * PQ), bf16),
             pltpu.VMEM((QR, QR), bf16), pltpu.VMEM((QR, QR), bf16),
             pltpu.VMEM(sums, f32), pltpu.VMEM(sums, f32), pltpu.VMEM(sums, f32),
-            dma((P_HERE,)), dma((7,)), dma((P_HERE + 1,)), dma((2, P_HERE)), dma((2, P_HERE)), dma((2,)),
+            dma((P_HERE,)), dma((7,)), dma((2, P_HERE)), dma((2, P_HERE)), dma((2,)),
             dma((2,)), dma((2,)), dma((2,)), dma((2,)), dma((2,)),
         ],
         compiler_params=pltpu.CompilerParams(collective_id=0, has_side_effects=True,
-                                             vmem_limit_bytes=60 * 1024 * 1024),
+                                             vmem_limit_bytes=40 * 1024 * 1024),
         cost_estimate=pl.CostEstimate(flops=600_000_000, bytes_accessed=3_000_000, transcendentals=0),
-    )(
+    )(*(pltpu.with_memory_space_constraint(a, pltpu.HBM) for a in (
         density.reshape(whole), velocity, shear_rates, hermite_matrix, laguerre_matrix,
         flow_first.transpose(1, 0, 2).reshape(flows), flow_second.transpose(1, 0, 2).reshape(flows),
         stress_weights.transpose(1, 2, 0, 3),
-    )
+    )))
     return advanced.reshape(density.shape), stress
 
 

time: 34.5 us -> 32.5 us (0.942)
  local copies, waits for them, and re-layouts: 2.84 us -> 1.55 us
  Pallas kernels: 30.8 us -> 30.1 us
    unnamed x4 -> x2, local copies, waits for them, and re-layouts: 2.84 us -> 1.55 us
    pallas_call x1, Pallas kernels: 30.8 us -> 30.1 us  [body(): pl.pallas_call(functools.partial(kernel, nx, ny), out_shape=results, in_s...]
where the time goes in v4:
time: 32.5 us; the launch traced here: 32.3 us
  Pallas kernels  30.1 us (93%)
  local copies, waits for them, and re-layouts  1.55 us (5%)
  between operations  0.64 us (2%)
    pallas_call x1, Pallas kernels, body(): pl.pallas_call(functools.partial(kernel, nx, ny), out_shape=results, in_s...  30.1 us
    unnamed x2, local copies, waits for them, and re-layouts  1.55 us

profile of v4, /device:TPU:0, one launch (start us, length us, event | category | flops | bytes accessed | tf_op | source)
XLA Modules:
  0.0 32.3 jit_solution(12919434714132746842)
XLA Ops:
  0.6 30.1 %shard_map.95 = (f32[2000,128]{1,0:T(8,128)S(1)}, f32[3,4,128]{2,1,0:T(4,128)S(1)}) custom-call(f32[2000,128]{1,0:T(8,128)} %bitcast.10, f32[2,4,128]{2,1,0:T(4,128)} %vel_hbm.1, f32[4,4,128]{2,1,0:T(4,128)} %shear_hbm.1, f32[10,10]{1,0:T(8,128)} %herm_hbm.1, f32[10,10]{1,0:T(8,128)} %lag_hbm.1, f32[40,10]{1,0:T(8,128)} %bitcast.12, f32[40,10]{1,0:T(8,128)} %bitcast.13, ...), custom_call_target="tpu_custom_call" | custom-call | flops 600000000 | bytes 3000000 | tf_op jit(solution)/shard_map/pallas_call | solution.py:301
  30.8 1.0 %copy.12 = f32[5,10,10,4,128]{4,3,2,1,0:T(4,128)} copy(f32[5,10,10,4,128]{4,3,2,1,0:T(4,128)S(1)} %bitcast.9) | data formatting | bytes 2048000
  31.7 0.6 %copy.13 = f32[3,4,128]{2,1,0:T(4,128)} copy(f32[3,4,128]{2,1,0:T(4,128)S(1)} %get-tuple-element.7) | data formatting | bytes 12288
